TPU v7x, 128 devices: a whole 4x4x4 slice. The times are simulated.
128 devices in a mesh: req: 8 (over x, core), exp: 16 (over y, z).
Axes of the slice: x: 4, y: 4, z: 4, core: 2. Of those that a mesh axis runs over, the one named last changes fastest.
Arguments:
- tokens: bfloat16 [8320, 2048], P('req'), may hold values from -6 to 6
- attn_gain: bfloat16 [2048], replicated, may hold values from 0.099609375 to 1.8984375
- wq_nope: bfloat16 [2048, 2048], P(None, 'exp'), may hold values from -0.125 to 0.125
- wq_rope: bfloat16 [2048, 1024], P(None, 'exp'), may hold values from -0.125 to 0.125
- w_latent: bfloat16 [2048, 512], replicated, may hold values from -0.125 to 0.125
- w_krope: bfloat16 [2048, 64], replicated, may hold values from -0.125 to 0.125
- latent_gain: bfloat16 [512], replicated, may hold values from 0.099609375 to 1.8984375
- w_uk: bfloat16 [512, 2048], P(None, 'exp'), may hold values from -0.25 to 0.25
- w_uv: bfloat16 [512, 2048], P(None, 'exp'), may hold values from -0.25 to 0.25
- w_out: bfloat16 [2048, 2048], P('exp'), may hold values from -0.125 to 0.125
- moe_gain: bfloat16 [2048], replicated, may hold values from 0.099609375 to 1.8984375
- w_router: bfloat16 [2048, 64], replicated, may hold values from -0.125 to 0.125
- w_gate: bfloat16 [128, 2048, 704], P(('req', 'exp')), may hold values from -0.125 to 0.125
- w_up: bfloat16 [128, 2048, 704], P(('req', 'exp')), may hold values from -0.125 to 0.125
- w_down: bfloat16 [128, 704, 2048], P(('req', 'exp')), may hold values from -0.15625 to 0.15625
- routes: int32 [8320, 6], P(('req', 'exp')), may hold values from 0 to 63, all different within a row; in each aligned block of 65 rows (0 to 64, 65 to 129, ...) at most 10 rows name the same one
- cache_latent: bfloat16 [128, 16, 32, 512], P('req', 'exp'), may hold values from -300 to 300
- cache_rope: bfloat16 [128, 16, 2048], P('req', 'exp'), may hold values from -6 to 6
- mig_dest: int32 [128], P('req'), may hold values from 0 to 7, as said below
- page_table: int32 [128, 16], P('req'), may hold values from 0 to 15, each once within a row
- cache_len: int32 [128], P('req'), may hold values from 1 to 512
- span_slot: int32 [8], P('req'), may hold values from 0 to 15
Outputs:
- mixed: bfloat16 [8320, 2048], P(('req', 'exp'))
Inputs may be any that keep to these rules, and one draw needn't show every extreme that they name: `routes`: among the rows of one device, no expert is named by more than 10 rows, a bound that some block reaches. `mig_dest`: among the 16 slots of each group, exactly 2 go to each group, itself included.
All inputs are finite; a program needn't handle non-finite values.
Results may differ from a plain program's by a relative error of at most 0.019.
The roundings to bfloat16 on the way count: a program that leaves them out, or rounds other values in their place, can miss the bound.
Values may be sent and summed in bfloat16 or wider, within the bound.
No kernel may reach another device: no remote copies, remote signals or barrier semaphores. Data moves between devices by JAX's collectives and lax.ppermute only.
A program may use at most 128 MiB of HBM per device.

v0:
```python
import math
import jax
import jax.numpy as jnp
from jax import lax
from jax.sharding import PartitionSpec as P

DN = 128
DR = 64
TOP = 6
SPAN = 1024
theta_base = 50000.0
route_scale = 2.446
norm_eps = 1e-06


def rms_scale(values, gain_values):
    widened = values.astype(jnp.float32)
    mean_square = jnp.mean(widened * widened, axis=-1, keepdims=True)
    return widened * lax.rsqrt(mean_square + norm_eps) * gain_values.astype(jnp.float32)


def rope_angles(positions, rope_width):
    exponent = jnp.arange(rope_width // 2, dtype=jnp.float32) * (2.0 / rope_width)
    frequency = jnp.exp(-exponent * math.log(theta_base))
    return positions.astype(jnp.float32)[:, None] * frequency[None, :]


def rotate(values, angles):
    half_width = values.shape[-1] // 2
    cosine = jnp.cos(angles)
    sine_part = jnp.sin(angles)
    first_half = values[..., :half_width]
    second_half = values[..., half_width:]
    return jnp.concatenate(
        [
            first_half * cosine - second_half * sine_part,
            second_half * cosine + first_half * sine_part,
        ],
        axis=-1,
    )


def group_positions(lengths, span_slots, span_width):
    starts = jnp.take(lengths, span_slots)
    span_positions = starts[:, None] + jnp.arange(span_width, dtype=jnp.int32)[None, :]
    return jnp.concatenate([span_positions.reshape(-1), lengths])


def dot_transposed(left_side, right_side):
    return lax.dot_general(
        left_side, right_side, (((1,), (1,)), ((), ())), preferred_element_type=jnp.float32
    )


def soft_weights(scores, visible):
    masked = jnp.where(visible, scores, -jnp.inf)
    row_top = jnp.max(masked, axis=-1, keepdims=True)
    raised = jnp.where(visible, jnp.exp(masked - row_top), 0.0)
    return (raised / jnp.sum(raised, axis=-1, keepdims=True)).astype(jnp.bfloat16)


def attend_head(
    query_latent,
    query_rope,
    new_latent,
    new_rope,
    cache_keys,
    cache_rope_keys,
    lengths,
    span_slots,
    span_width,
    scale_factor,
):
    cache_size = cache_keys.shape[1]
    key_index = jnp.arange(cache_size + span_width, dtype=jnp.int32)
    row_index = jnp.arange(span_width, dtype=jnp.int32)
    results = []
    request = span_slots[0]
    keys_latent = jnp.concatenate([cache_keys[request], new_latent[0:span_width]], axis=0)
    keys_rope = jnp.concatenate([cache_rope_keys[request], new_rope[0:span_width]], axis=0)
    scores = (
        dot_transposed(query_latent[0:span_width], keys_latent)
        + dot_transposed(query_rope[0:span_width], keys_rope)
    ) * scale_factor
    visible = jnp.where(
        key_index[None, :] < cache_size,
        key_index[None, :] < lengths[request],
        key_index[None, :] - cache_size <= row_index[:, None],
    )
    weights = soft_weights(scores, visible)
    results.append(
        jnp.dot(weights, keys_latent, preferred_element_type=jnp.float32).astype(jnp.bfloat16)
    )
    dec_start = span_slots.shape[0] * span_width
    dec_latent = query_latent[dec_start:]
    dec_rope = query_rope[dec_start:]
    own_latent = new_latent[dec_start:]
    own_rope = new_rope[dec_start:]
    cache_scores = (
        jnp.einsum("jr,jpr->jp", dec_latent, cache_keys, preferred_element_type=jnp.float32)
        + jnp.einsum("je,jpe->jp", dec_rope, cache_rope_keys, preferred_element_type=jnp.float32)
    ) * scale_factor
    self_scores = (
        jnp.sum(dec_latent.astype(jnp.float32) * own_latent.astype(jnp.float32), axis=1)
        + jnp.sum(dec_rope.astype(jnp.float32) * own_rope.astype(jnp.float32), axis=1)
    ) * scale_factor
    seen = jnp.arange(cache_size, dtype=jnp.int32)[None, :] < lengths[:, None]
    masked = jnp.where(seen, cache_scores, -jnp.inf)
    row_top = jnp.maximum(jnp.max(masked, axis=1), self_scores)
    cache_raised = jnp.where(seen, jnp.exp(masked - row_top[:, None]), 0.0)
    self_raised = jnp.exp(self_scores - row_top)
    totals = jnp.sum(cache_raised, axis=1) + self_raised
    cache_weights = (cache_raised / totals[:, None]).astype(jnp.bfloat16)
    self_weights = (self_raised / totals).astype(jnp.bfloat16)
    dec_out = jnp.einsum(
        "jp,jpr->jr", cache_weights, cache_keys, preferred_element_type=jnp.float32
    ) + self_weights.astype(jnp.float32)[:, None] * own_latent.astype(jnp.float32)
    results.append(dec_out.astype(jnp.bfloat16))
    return jnp.concatenate(results, axis=0)


def one_half(inputs, gate_part, up_part, down_part):
    hidden = (
        jax.nn.silu(jnp.dot(inputs, gate_part, preferred_element_type=jnp.float32))
        * jnp.dot(inputs, up_part, preferred_element_type=jnp.float32)
    ).astype(jnp.bfloat16)
    return jnp.dot(hidden, down_part, preferred_element_type=jnp.float32).astype(jnp.bfloat16)


def expert_halves(received, w_gate, w_up, w_down):
    sources, halves, slot_count, model_width = received.shape
    inputs = received[:, 0].reshape(sources * slot_count, model_width)
    output = one_half(inputs, w_gate[0], w_up[0], w_down[0])
    results = [output.reshape(sources, slot_count, model_width)]
    return jnp.stack(results, axis=1)


def shards(
    tokens,
    attn_gain,
    wq_nope,
    wq_rope,
    w_latent,
    w_krope,
    latent_gain,
    w_uk,
    w_uv,
    w_out,
    moe_gain,
    w_router,
    w_gate,
    w_up,
    w_down,
    routes,
    cache_latent,
    cache_rope,
    mig_dest,
    page_table,
    cache_len,
    span_slot,
):
    req_count = lax.axis_size("req")
    exp_count = lax.axis_size("exp")
    device_count = req_count * exp_count
    req_group = mig_dest.shape[0]
    move_count = req_group // req_count
    rows_group = tokens.shape[0]
    rows_device = rows_group // exp_count
    model_width = tokens.shape[1]
    heads_device = wq_nope.shape[1] // DN
    scale_factor = 1.0 / math.sqrt(DN + DR)
    slot_ids = jnp.arange(req_group, dtype=jnp.int32)
    earlier = (mig_dest[None, :] == mig_dest[:, None]) & (slot_ids[None, :] < slot_ids[:, None])
    placed = mig_dest * move_count + jnp.sum(earlier.astype(jnp.int32), axis=1)
    source_slot = jnp.argmax((placed[None, :] == slot_ids[:, None]).astype(jnp.int32), axis=1)
    outgoing_latent = cache_latent[source_slot].reshape(
        (req_count, move_count) + cache_latent.shape[1:]
    )
    outgoing_rope = cache_rope[source_slot].reshape((req_count, move_count) + cache_rope.shape[1:])
    arrived = (
        lax.all_to_all(outgoing_latent, "req", split_axis=0, concat_axis=0, tiled=True),
        lax.all_to_all(outgoing_rope, "req", split_axis=0, concat_axis=0, tiled=True),
    )
    local_latent = arrived[0].reshape(cache_latent.shape)
    local_rope = arrived[1].reshape(cache_rope.shape)
    whole_latent, whole_rope = (
        lax.all_gather(local_latent, "exp", axis=1, tiled=True),
        lax.all_gather(local_rope, "exp", axis=1, tiled=True),
    )
    cache_keys = jnp.take_along_axis(whole_latent, page_table[:, :, None, None], axis=1).reshape(
        req_group, -1, whole_latent.shape[-1]
    )
    cache_rope_keys = jnp.take_along_axis(whole_rope, page_table[:, :, None], axis=1).reshape(
        req_group, -1, DR
    )
    normed = rms_scale(tokens, attn_gain).astype(jnp.bfloat16)
    angles = rope_angles(group_positions(cache_len, span_slot, SPAN), DR)
    query_nope = jnp.dot(normed, wq_nope, preferred_element_type=jnp.float32).astype(jnp.bfloat16)
    query_rope = rotate(
        jnp.dot(normed, wq_rope, preferred_element_type=jnp.float32).reshape(
            rows_group, heads_device, DR
        ),
        angles[:, None, :],
    ).astype(jnp.bfloat16)
    row_offset = lax.axis_index("exp") * rows_device
    own_normed = lax.dynamic_slice_in_dim(normed, row_offset, rows_device, 0)
    own_angles = lax.dynamic_slice_in_dim(angles, row_offset, rows_device, 0)
    own_latent = rms_scale(
        jnp.dot(own_normed, w_latent, preferred_element_type=jnp.float32), latent_gain
    ).astype(jnp.bfloat16)
    own_rope = rotate(
        jnp.dot(own_normed, w_krope, preferred_element_type=jnp.float32), own_angles
    ).astype(jnp.bfloat16)
    new_latent, new_rope = (
        lax.all_gather(own_latent, "exp", axis=0, tiled=True),
        lax.all_gather(own_rope, "exp", axis=0, tiled=True),
    )
    query_latent = dot_transposed(query_nope, w_uk).astype(jnp.bfloat16)
    attended = attend_head(
        query_latent,
        query_rope[:, 0],
        new_latent,
        new_rope,
        cache_keys,
        cache_rope_keys,
        cache_len,
        span_slot,
        SPAN,
        scale_factor,
    )
    head_outs = jnp.dot(attended, w_uv, preferred_element_type=jnp.float32).astype(jnp.bfloat16)
    attn_rows = lax.psum_scatter(
        jnp.dot(head_outs, w_out, preferred_element_type=jnp.float32).astype(jnp.bfloat16),
        "exp",
        scatter_dimension=0,
        tiled=True,
    ).astype(jnp.float32)
    own_tokens = lax.dynamic_slice_in_dim(tokens, row_offset, rows_device, 0)
    resid = (own_tokens.astype(jnp.float32) + attn_rows).astype(jnp.bfloat16)
    moe_in = rms_scale(resid, moe_gain).astype(jnp.bfloat16)
    picked = jnp.take_along_axis(
        jax.nn.sigmoid(jnp.dot(moe_in, w_router, preferred_element_type=jnp.float32)),
        routes,
        axis=1,
    )
    gate_w = route_scale * picked / jnp.sum(picked, axis=1, keepdims=True)
    expert_count = w_router.shape[1]
    capacity = 2 * ((rows_device * TOP // expert_count + 5) // 2)
    flat_routes = routes.reshape(-1)
    onehot = (flat_routes[:, None] == jnp.arange(expert_count, dtype=jnp.int32)[None, :]).astype(
        jnp.int32
    )
    slot_rank = jnp.sum((jnp.cumsum(onehot, axis=0) - 1) * onehot, axis=1)
    slot_of = flat_routes * capacity + slot_rank
    slot_index = jnp.arange(expert_count * capacity, dtype=jnp.int32)
    dispatch_rows = jnp.any(
        (slot_of[None, :] == slot_index[:, None]).reshape(
            expert_count * capacity, rows_device, TOP
        ),
        axis=2,
    ).astype(jnp.bfloat16)
    packed = jnp.dot(dispatch_rows, moe_in, preferred_element_type=jnp.float32).astype(jnp.bfloat16)
    halves_device = w_gate.shape[0]
    doubled = jnp.broadcast_to(
        packed.reshape(expert_count, 1, capacity, model_width),
        (expert_count, 2, capacity, model_width),
    ).reshape(device_count, halves_device, capacity, model_width)
    computed = expert_halves(
        lax.all_to_all(doubled, ("req", "exp"), split_axis=0, concat_axis=0, tiled=True),
        w_gate,
        w_up,
        w_down,
    )
    returned = lax.all_to_all(computed, ("req", "exp"), split_axis=0, concat_axis=0, tiled=True)
    paired = returned.reshape(expert_count, 2, capacity, model_width)
    expert_out = (
        (paired[:, 0].astype(jnp.float32) + paired[:, 1].astype(jnp.float32))
        .astype(jnp.bfloat16)
        .reshape(expert_count * capacity, model_width)
    )
    gathered = expert_out[slot_of].astype(jnp.float32).reshape(rows_device, TOP, model_width)
    moe_out = jnp.sum(gate_w[:, :, None] * gathered, axis=1)
    return (resid.astype(jnp.float32) + moe_out).astype(jnp.bfloat16)


def solution(mesh):
    in_specs = (
        P("req", None),
        P(),
        P(None, "exp"),
        P(None, "exp"),
        P(),
        P(),
        P(),
        P(None, "exp"),
        P(None, "exp"),
        P("exp", None),
        P(),
        P(),
        P(("req", "exp"), None, None),
        P(("req", "exp"), None, None),
        P(("req", "exp"), None, None),
        P(("req", "exp"), None),
        P("req", "exp", None, None),
        P("req", "exp", None),
        P("req"),
        P("req", None),
        P("req"),
        P("req"),
    )
    out_specs = P(("req", "exp"), None)
    return jax.shard_map(shards, mesh=mesh, in_specs=in_specs, out_specs=out_specs, check_vma=False)
```

profile of v0, /device:TPU:8, one launch (start us, length us, event | category | flops | bytes accessed | tf_op | source)
XLA Modules:
  0.0 632.7 jit_solution(2216624026873869297)
XLA Ops:
  6.5 0.8 convert_element_type.149
  7.4 3.1 fusion.1
  10.6 5.2 fusion.3
  15.9 2.3 multiply_reduce_fusion.1
  18.1 0.7 fusion.51
  20.5 9.7 %all_to_all.20 = bf16[8,2,1,2048]{3,1,2,0:T(2,128)(2,1)S(1)} all-to-all(bf16[8,2,1,2048]{3,1,2,0:T(2,128)(2,1)S(1)} %bitcast.125), channel_id=1, replica_groups=mesh['req'=8,'exp'=16] {'req'}, dimensions={0} | all-to-all | bytes 131072 | tf_op jit(solution)/shard_map/all_to_all | solution.py:182
  30.9 1.6 gather_fusion
  32.6 13.5 %all_to_all.21 = bf16[8,2,1,32,512]{4,3,1,2,0:T(8,128)(2,1)} all-to-all(bf16[8,2,1,32,512]{4,3,1,2,0:T(8,128)(2,1)S(1)} %bitcast.122), channel_id=1, replica_groups=mesh['req'=8,'exp'=16] {'req'}, dimensions={0} | all-to-all | bytes 1048576 | tf_op jit(solution)/shard_map/all_to_all | solution.py:181
  46.4 1.2 reduce-window.6
  50.6 1.4 fusion.29
  52.2 24.8 %all-gather.1 = bf16[16,65,64]{1,2,0:T(8,128)(2,1)S(1)} all-gather(bf16[1,65,64]{1,2,0:T(8,128)(2,1)S(1)} %maximum_bitcast_fusion), channel_id=1, replica_groups=mesh['req'=8,'exp'=16] {'exp'}, dimensions={0}, use_global_device_ids=true | all-gather | bytes 141440 | tf_op jit(solution)/shard_map/all_gather | solution.py:216
  77.4 3.7 convolution_bitcast_fusion
  81.9 0.7 iota_compare_fusion.7
  82.6 5.3 convolution_convert_fusion.3
  88.0 0.7 slice_bitcast_fusion.2
  88.7 2.4 reshape.471
  91.1 2.3 slice.94
  93.4 0.9 fusion.52
  94.2 14.4 %all-gather.8.cloned.1.call-done = bf16[16,16,2048]{2,0,1:T(8,128)(2,1)} async-done(((bf16[16,1,2048]{2,0,1:T(8,128)(2,1)}), bf16[16,16,2048]{2,0,1:T(8,128)(2,1)}) %all-gather.8.cloned.1.call-update) | async-done | bytes 1048592 | tf_op jit(solution)/shard_map/all_gather | solution.py:188
  108.6 2.8 copy.77
  111.4 5.1 gather_fusion.4
  116.6 4.4 gather.35
  121.0 3.2 broadcast_select_fusion
  124.2 1.4 copy-done.1
  125.7 2.2 fusion.87
  128.0 53.3 %all-gather.6.cloned.1.call-done = bf16[16,16,32,512]{3,2,0,1:T(8,128)(2,1)} async-done(((bf16[16,1,32,512]{3,2,0,1:T(8,128)(2,1)}), bf16[16,16,32,512]{3,2,0,1:T(8,128)(2,1)}) %all-gather.6.cloned.1.call-update) | async-done | bytes 8388624 | tf_op jit(solution)/shard_map/all_gather | solution.py:187
  181.3 13.4 %gather_fusion.3 = bf16[256,32,512]{2,1,0:T(8,128)(2,1)} fusion(bf16[16,16,32,512]{3,2,0,1:T(8,128)(2,1)} %all-gather.6.cloned.1.call-done, s32[256]{0:T(256)S(1)} %reshape.436), kind=kCustom, calls=%fused_computation.3 | custom fusion | bytes 16779264 | tf_op jit(solution)/shard_map/jit(take_along_axis)/gather | solution.py:190
  194.7 4.9 bitcast_select_fusion
  199.7 2.3 fusion.59
  202.5 1.2 fusion.57
  204.0 1.8 fusion.23
  205.8 2.3 fusion.86
  208.1 2.1 fusion.5
  210.2 3.4 fusion.12
  213.6 0.8 fusion.54
  214.4 5.1 convolution_convert_fusion.1
  219.6 66.6 %fusion = bf16[80,2048]{1,0:T(8,128)(2,1)S(1)} fusion(bf16[1040,2048]{1,0:T(8,128)(2,1)} %convolution_convert_fusion.1), kind=kCustom, calls=%all-reduce-scatter | all-reduce-scatter fusion | flops 2621441 | bytes 4588032
  286.2 0.8 slice.109
  287.0 3.4 collective-permute-start.1
  290.4 1.9 collective-permute-start
  292.3 3.9 collective-permute-start.2
  297.9 4.2 collective-permute-done.2
  302.2 6.0 collective-permute-done
  308.1 11.8 %concatenate.48 = bf16[305,2048]{1,0:T(8,128)(2,1)} concatenate(bf16[65,2048]{1,0:T(8,128)(2,1)} %collective-permute-done.2, bf16[80,2048]{1,0:T(8,128)(2,1)} %collective-permute-done.1, bf16[80,2048]{1,0:T(8,128)(2,1)} %collective-permute-done, bf16[80,2048]{1,0:T(8,128)(2,1)S(1)} %fusion), dimensions={0} | concatenate | bytes 2498560
  319.9 1.4 fusion.25
  321.3 2.5 convolution_convert_fusion.2
  323.7 5.4 broadcast_in_dim.120
  329.1 6.8 %broadcast_in_dim.121 = bf16[64,2,10,2048]{3,2,1,0:T(8,128)(2,1)} broadcast(bf16[64,10,2048]{2,1,0:T(8,128)(2,1)} %broadcast_in_dim.120), dimensions={0,2,3} | broadcast | bytes 7864320 | tf_op jit(solution)/shard_map/broadcast_in_dim | solution.py:264
  335.9 110.3 %all_to_all.22 = bf16[128,1,10,2048]{3,2,1,0:T(8,128)(2,1)} all-to-all(bf16[128,1,10,2048]{3,2,1,0:T(8,128)(2,1)} %bitcast.119), channel_id=1, replica_groups=mesh['req'=8,'exp'=16] {'req','exp'}, dimensions={0} | all-to-all | bytes 10485760 | tf_op jit(solution)/shard_map/all_to_all | solution.py:269
  446.2 9.8 %reshape_squeeze.3 = bf16[1280,2048]{1,0:T(8,128)(2,1)} reshape(bf16[128,1,10,2048]{3,2,1,0:T(8,128)(2,1)} %all_to_all.22) | data formatting | bytes 10485760 | tf_op jit(solution)/shard_map/reshape;squeeze | solution.py:132
  456.0 7.4 %fusion.10 = f32[1280,704]{0,1:T(8,128)S(1)} fusion(bf16[1280,2048]{1,0:T(8,128)(2,1)} %reshape_squeeze.3, bf16[1,2048,704]{1,2,0:T(8,128)(2,1)} %param.34), kind=kOutput, calls=%fused_computation.31 | convolution fusion | flops 3690987520 | bytes 11730944 | tf_op jit(solution)/shard_map/dot_general | solution.py:124
  463.5 4.2 fusion.6
  467.7 6.1 convolution_convert_fusion
  473.8 9.5 %stack_reshape.3 = bf16[128,1,10,2048]{3,2,0,1:T(8,128)(2,1)} reshape(bf16[1280,2048]{1,0:T(8,128)(2,1)} %convolution_convert_fusion) | data formatting | bytes 10485760 | tf_op jit(solution)/shard_map/stack;reshape | solution.py:135
  483.3 6.1 all-to-all-start.3
  489.9 1.3 fusion.15
  491.2 4.8 gather_fusion.5
  496.3 102.8 %all-to-all-done.3 = bf16[128,1,10,2048]{3,2,1,0:T(8,128)(2,1)} async-done(((bf16[128,1,10,2048]{3,2,1,0:T(8,128)(2,1)}), bf16[128,1,10,2048]{3,2,1,0:T(8,128)(2,1)}, u32[]{:S(2)}, u32[]{:S(2)}) %all-to-all-start.3) | async-done | bytes 5242912 | tf_op jit(solution)/shard_map/all_to_all | solution.py:274
  599.1 5.7 add_convert_fusion
  604.8 5.5 convert_element_type.181
  610.3 7.2 %gather_fusion.2 = bf16[390,2048]{1,0:T(8,128)(2,1)} fusion(bf16[640,2048]{1,0:T(8,128)(2,1)} %convert_element_type.181, s32[1024]{0:T(1024)S(1)} %pad_clamp_fusion), kind=kCustom, calls=%fused_computation.2 | custom fusion | bytes 3196440 | tf_op jit(solution)/shard_map/gather | solution.py:281
  617.5 3.9 reshape.400
  621.4 3.8 multiply_reduce_fusion
  625.2 0.8 fusion.28
  (105 shorter events, 8.3 us)
Async XLA Ops:
  6.5 461.2 %copy-start = (bf16[1,704,2048]{2,1,0:T(8,128)(2,1)S(1)}, bf16[1,704,2048]{2,1,0:T(8,128)(2,1)}, u32[]{:S(2)}) copy-start(bf16[1,704,2048]{2,1,0:T(8,128)(2,1)} %param.36) | copy-start | bytes 8650756
  6.5 4.0 copy-start.12
  6.5 82.1 %all-gather.10.cloned.1.call-start = ((), (), s32[]{:S(2)}) async-start(), calls=%async_computation.6 | async-start | bytes 1253376 | tf_op jit(solution)/shard_map/all_gather | solution.py:215
  10.6 8.4 %copy-start.15 = (s32[16]{0:T(128)S(1)}, s32[16]{0:T(128)}, u32[]{:S(2)}) copy-start(s32[16]{0:T(128)} %param.40) | copy-start | bytes 196
  10.6 9.2 %copy-start.3 = (bf16[16,1,2048]{2,0,1:T(8,128)(2,1)S(1)}, bf16[16,1,2048]{2,0,1:T(8,128)(2,1)}, u32[]{:S(2)}) copy-start(bf16[16,1,2048]{2,0,1:T(8,128)(2,1)} %param.39) | copy-start | bytes 196612
  15.8 30.2 %copy-start.8 = (s32[65,6]{0,1:T(8,128)S(1)}, s32[65,6]{0,1:T(8,128)}, u32[]{:S(2)}) copy-start(s32[65,6]{0,1:T(8,128)} %param.37) | copy-start | bytes 4684
  15.9 32.3 %copy-start.9 = (s32[16,16]{1,0:T(8,128)S(1)}, s32[16,16]{1,0:T(8,128)}, u32[]{:S(2)}) copy-start(s32[16,16]{1,0:T(8,128)} %param.41) | copy-start | bytes 3076
  15.9 33.3 %copy-start.10 = (s32[16]{0:T(128)S(1)}, s32[16]{0:T(128)}, u32[]{:S(2)}) copy-start(s32[16]{0:T(128)} %param.42) | copy-start | bytes 196
  18.9 89.7 %all-gather.8.cloned.1.call-start = ((), (), s32[]{:S(2)}) async-start(), calls=%async_computation.5 | async-start | bytes 1114112 | tf_op jit(solution)/shard_map/all_gather | solution.py:188
  30.9 150.4 %all-gather.6.cloned.1.call-start = ((), (), s32[]{:S(2)}) async-start(), calls=%async_computation.4 | async-start | bytes 8912896 | tf_op jit(solution)/shard_map/all_gather | solution.py:187
  77.4 10.5 %copy-start.6 = (bf16[1040,64]{0,1:T(8,128)(2,1)}, bf16[1040,64]{0,1:T(8,128)(2,1)S(1)}, u32[]{:S(2)}) copy-start(bf16[1040,64]{0,1:T(8,128)(2,1)S(1)} %reshape.473) | copy-start | bytes 399364
  124.2 1.4 copy-start.1
  202.4 1.2 copy-start.4
  202.4 1.5 copy-start.5
  204.0 1.8 slice-start
  210.2 4.2 copy-start.7
  214.4 81.9 %copy-start.11 = (bf16[2048]{0:T(1024)(128)(2,1)S(1)}, bf16[2048]{0:T(1024)(128)(2,1)}, u32[]{:S(2)}) copy-start(bf16[2048]{0:T(1024)(128)(2,1)} %param.32) | copy-start | bytes 12292
  214.4 81.9 %copy-start.13 = (u32[128]{0:T(128)S(1)}, u32[128]{0:T(128)}, u32[]{:S(2)}) copy-start(u32[128]{0:T(128)} %constant.195) | copy-start | bytes 1540
  287.0 15.2 %collective-permute-start.1 = (bf16[80,2048]{1,0:T(8,128)(2,1)S(1)}, bf16[80,2048]{1,0:T(8,128)(2,1)}, u32[]{:S(2)}, u32[]{:S(2)}) collective-permute-start(bf16[80,2048]{1,0:T(8,128)(2,1)S(1)} %fusion), channel_id=1, source_target_pairs={{0,2},{1,3},{2,4},{3,5},{4,6},{5,7},{6,8},{7,9},{8,10},{9,11},{10,... | collective-permute-start | bytes 983048
  290.4 17.7 %collective-permute-start = (bf16[80,2048]{1,0:T(8,128)(2,1)S(1)}, bf16[80,2048]{1,0:T(8,128)(2,1)}, u32[]{:S(2)}, u32[]{:S(2)}) collective-permute-start(bf16[80,2048]{1,0:T(8,128)(2,1)S(1)} %fusion), channel_id=1, source_target_pairs={{0,1},{1,2},{2,3},{3,4},{4,5},{5,6},{6,7},{7,8},{8,9},{9,10},{10,1... | collective-permute-start | bytes 983048
  292.3 9.8 %collective-permute-start.2 = (bf16[65,2048]{1,0:T(8,128)(2,1)}, bf16[65,2048]{1,0:T(8,128)(2,1)}, u32[]{:S(2)}, u32[]{:S(2)}) collective-permute-start(bf16[65,2048]{1,0:T(8,128)(2,1)} %slice.109), channel_id=1, source_target_pairs={{0,3},{1,4},{2,5},{3,6},{4,7},{5,8},{6,9},{7,10},{8,11},{9,12},{10... | collective-permute-start | bytes 798728
  456.0 7.5 %copy-start.2 = (bf16[1280,2048]{1,0:T(8,128)(2,1)S(1)}, bf16[1280,2048]{1,0:T(8,128)(2,1)}, u32[]{:S(2)}) copy-start(bf16[1280,2048]{1,0:T(8,128)(2,1)} %reshape_squeeze.3) | copy-start | bytes 15728644
  456.0 7.5 %copy-start.14 = (bf16[1,2048,704]{1,2,0:T(8,128)(2,1)S(1)}, bf16[1,2048,704]{1,2,0:T(8,128)(2,1)}, u32[]{:S(2)}) copy-start(bf16[1,2048,704]{1,2,0:T(8,128)(2,1)} %param.35) | copy-start | bytes 8650756
  483.3 115.7 %all-to-all-start.3 = ((bf16[128,1,10,2048]{3,2,1,0:T(8,128)(2,1)}), bf16[128,1,10,2048]{3,2,1,0:T(8,128)(2,1)}, u32[]{:S(2)}, u32[]{:S(2)}) async-start(bf16[128,1,10,2048]{3,2,1,0:T(8,128)(2,1)} %bitcast.117), calls=%async_computation.3 | async-start | bytes 16777216 | tf_op jit(solution)/shard_map/all_to_all | solution.py:274
Sparse Core Ops, SparseCore 0:
  19.0 45.2 all-gather.9
  66.4 42.1 all-gather.7
  110.8 70.4 all-gather.5
where the time goes:
time: 641 us; the launch traced here: 633 us
  blocking collectives  225 us (35%)
  waiting for transfers between devices  181 us (28%)
  local copies, waits for them, and re-layouts  105 us (16%)
  matrix products  52.5 us (8%)
  other arithmetic  38.1 us (6%)
  between operations  15.9 us (2%)
  starting transfers between devices  15.5 us (2%)
    all_to_all x1, blocking collectives, shards(): lax.all_to_all(doubled, ('req', 'exp'), split_axis=0, concat_axis=0, tile...  110 us
    all_to_all x1, waiting for transfers between devices, shards(): lax.all_to_all(computed, ('req', 'exp'), split_axis=0, concat_axis=0, til...  103 us
    unnamed x1, blocking collectives  66.6 us
    all_gather x1, waiting for transfers between devices, shards(): lax.all_gather(local_latent, 'exp', axis=1, tiled=True)  53.3 us
    all_gather x1, blocking collectives, shards(): lax.all_gather(own_rope, 'exp', axis=0, tiled=True)  24.8 us
    unnamed x38, local copies, waits for them, and re-layouts  17.8 us
    all_gather x1, waiting for transfers between devices, shards(): lax.all_gather(local_rope, 'exp', axis=1, tiled=True)  14.4 us
    gather x2, local copies, waits for them, and re-layouts, shards(): jnp.take_along_axis(whole_latent, page_table[:, :, None, None], axis=1)  13.5 us
  transfers between devices with their start and end apart: 7, of which 5 were waited for; matrix products, arithmetic and copies ran while one was open for 8% of the time, Pallas kernels for 0%

commit v1 on v0

--- a/solution.py
+++ b/solution.py
@@ -184,7 +184,9 @@
     local_latent = arrived[0].reshape(cache_latent.shape)
     local_rope = arrived[1].reshape(cache_rope.shape)
     whole_latent, whole_rope = (
-        lax.all_gather(local_latent, "exp", axis=1, tiled=True),
+        jnp.concatenate(
+            lax.all_to_all(jnp.stack([local_latent] * lax.axis_size("exp")), "exp", 0, 0), axis=1
+        ),
         lax.all_gather(local_rope, "exp", axis=1, tiled=True),
     )
     cache_keys = jnp.take_along_axis(whole_latent, page_table[:, :, None, None], axis=1).reshape(

time: 641 us -> 725 us (1.13)
  blocking collectives: 225 us -> 331 us
  waiting for transfers between devices: 181 us -> 137 us
  starting transfers between devices: 15.5 us -> 28.3 us
  local copies, waits for them, and re-layouts: 105 us -> 115 us
    all_gather x1, blocking collectives: 24.8 us -> 141 us  [shards(): lax.all_gather(own_rope, 'exp', axis=0, tiled=True)]
    all_gather x1 -> x0, waiting for transfers between devices: 53.3 us -> none  [shards(): lax.all_gather(local_latent, 'exp', axis=1, tiled=True)]
    all_to_all x0 -> x2, starting transfers between devices: none -> 12.8 us  [the longest x1 8.54 us: shards(): lax.all_to_all(jnp.stack([local_latent] * lax.axis_size('exp')), 'exp', 0...]
    all_to_all x1 -> x0, blocking collectives: 9.72 us -> none  [shards(): lax.all_to_all(outgoing_rope, 'req', split_axis=0, concat_axis=0, tiled=T...]
    unnamed x38 -> x56, local copies, waits for them, and re-layouts: 17.8 us -> 20.7 us
  transfers between devices with their start and end apart: 7 -> 8, of which waited for: 5 -> 5; matrix products, arithmetic and copies ran while one was open for 8% -> 8% of each run, Pallas kernels for 0% -> 0%
where the time goes in v1:
time: 725 us; the launch traced here: 716 us
  blocking collectives  331 us (46%)
  waiting for transfers between devices  137 us (19%)
  local copies, waits for them, and re-layouts  115 us (16%)
  matrix products  50.6 us (7%)
  other arithmetic  38.1 us (5%)
  starting transfers between devices  28.3 us (4%)
  between operations  16.2 us (2%)
    all_gather x1, blocking collectives, shards(): lax.all_gather(own_rope, 'exp', axis=0, tiled=True)  141 us
    all_to_all x1, blocking collectives, shards(): lax.all_to_all(doubled, ('req', 'exp'), split_axis=0, concat_axis=0, tile...  110 us
    all_to_all x1, waiting for transfers between devices, shards(): lax.all_to_all(computed, ('req', 'exp'), split_axis=0, concat_axis=0, til...  103 us
    unnamed x1, blocking collectives  66.5 us
    unnamed x56, local copies, waits for them, and re-layouts  20.7 us
    all_gather x1, waiting for transfers between devices, shards(): lax.all_gather(local_rope, 'exp', axis=1, tiled=True)  20 us
  transfers between devices with their start and end apart: 8, of which 5 were waited for; matrix products, arithmetic and copies ran while one was open for 8% of the time, Pallas kernels for 0%

profile of v1, /device:TPU:8, one launch (start us, length us, event | category | flops | bytes accessed | tf_op | source)
XLA Modules:
  0.0 715.8 jit_solution(6303297692687082032)
XLA Ops:
  6.5 1.0 convert_reduce_fusion
  8.8 1.5 gather_fusion.1
  11.0 4.3 all-to-all-start.2
  15.3 1.6 gather_fusion
  17.0 4.0 all-to-all-done.2
  21.0 12.8 %all_to_all.25 = bf16[8,2,1,32,512]{4,3,1,2,0:T(8,128)(2,1)S(1)} all-to-all(bf16[8,2,1,32,512]{4,3,1,2,0:T(8,128)(2,1)S(1)} %bitcast.125), channel_id=1, replica_groups=mesh['req'=8,'exp'=16] {'req'}, dimensions={0} | all-to-all | bytes 1048576 | tf_op jit(solution)/shard_map/all_to_all | solution.py:181
  33.8 4.3 stack.3
  38.0 8.5 %all-to-all-start.1 = ((bf16[16,16,1,32,512]{4,3,2,1,0:T(8,128)(2,1)}), bf16[16,16,1,32,512]{4,3,2,1,0:T(8,128)(2,1)}, u32[]{:S(2)}, u32[]{:S(2)}) async-start(bf16[16,16,1,32,512]{4,3,2,1,0:T(8,128)(2,1)} %stack.3), calls=%async_computation.1 | async-start | bytes 16777216 | tf_op jit(solution)/shard_map/all_to_all | solution.py:188
  46.7 3.1 fusion.1
  49.8 3.4 fusion.3
  53.2 2.0 copy-done.1
  56.9 1.2 reduce-window.6
  60.8 1.4 fusion.85
  64.1 1.2 fusion.29
  66.2 141.5 %all-gather.1 = bf16[16,65,64]{1,2,0:T(8,128)(2,1)S(1)} all-gather(bf16[1,65,64]{1,2,0:T(8,128)(2,1)S(1)} %maximum_bitcast_fusion), channel_id=1, replica_groups=mesh['req'=8,'exp'=16] {'exp'}, dimensions={0}, use_global_device_ids=true | all-gather | bytes 141440 | tf_op jit(solution)/shard_map/all_gather | solution.py:218
  208.2 3.7 convolution_bitcast_fusion
  213.3 5.3 convolution_convert_fusion.3
  219.3 2.4 reshape.479
  221.7 2.3 slice.94
  224.0 0.9 fusion.52
  224.9 20.0 %all-gather.5.cloned.1.call-done = bf16[16,16,2048]{2,0,1:T(8,128)(2,1)} async-done(((bf16[16,1,2048]{2,0,1:T(8,128)(2,1)}), bf16[16,16,2048]{2,0,1:T(8,128)(2,1)}) %all-gather.5.cloned.1.call-update) | async-done | bytes 1048592 | tf_op jit(solution)/shard_map/all_gather | solution.py:190
  244.9 2.8 copy.77
  247.6 5.2 gather_fusion.4
  252.8 4.4 gather.35
  257.2 3.2 broadcast_select_fusion
  260.5 1.3 copy-done.2
  261.9 2.2 fusion.87
  264.1 13.5 %gather_fusion.3 = bf16[256,32,512]{2,1,0:T(8,128)(2,1)} fusion(bf16[16,16,32,512]{3,2,0,1:T(8,128)(2,1)} %bitcast.6, s32[256]{0:T(256)S(1)} %reshape.444), kind=kCustom, calls=%fused_computation.3 | custom fusion | bytes 16779264 | tf_op jit(solution)/shard_map/jit(take_along_axis)/gather | solution.py:192
  277.6 4.9 bitcast_select_fusion
  282.6 2.3 fusion.59
  285.4 1.2 fusion.57
  286.9 1.8 fusion.23
  288.7 2.3 fusion.86
  291.0 2.1 fusion.5
  293.1 3.4 fusion.12
  296.6 0.8 fusion.54
  297.4 5.1 convolution_convert_fusion.1
  302.5 66.5 %fusion = bf16[80,2048]{1,0:T(8,128)(2,1)S(1)} fusion(bf16[1040,2048]{1,0:T(8,128)(2,1)} %convolution_convert_fusion.1), kind=kCustom, calls=%all-reduce-scatter | all-reduce-scatter fusion | flops 2621441 | bytes 4588032
  369.8 3.4 collective-permute-start.1
  373.2 1.9 collective-permute-start
  375.2 3.9 collective-permute-start.2
  380.8 4.2 collective-permute-done.2
  385.0 6.0 collective-permute-done
  391.0 11.8 %concatenate.48 = bf16[305,2048]{1,0:T(8,128)(2,1)} concatenate(bf16[65,2048]{1,0:T(8,128)(2,1)} %collective-permute-done.2, bf16[80,2048]{1,0:T(8,128)(2,1)} %collective-permute-done.1, bf16[80,2048]{1,0:T(8,128)(2,1)} %collective-permute-done, bf16[80,2048]{1,0:T(8,128)(2,1)S(1)} %fusion), dimensions={0} | concatenate | bytes 2498560
  402.8 1.4 fusion.25
  404.1 2.5 convolution_convert_fusion.2
  406.6 5.4 broadcast_in_dim.120
  412.0 6.8 broadcast_in_dim.121
  418.7 110.3 %all_to_all.26 = bf16[128,1,10,2048]{3,2,1,0:T(8,128)(2,1)} all-to-all(bf16[128,1,10,2048]{3,2,1,0:T(8,128)(2,1)} %bitcast.122), channel_id=1, replica_groups=mesh['req'=8,'exp'=16] {'req','exp'}, dimensions={0} | all-to-all | bytes 10485760 | tf_op jit(solution)/shard_map/all_to_all | solution.py:271
  529.0 9.8 %reshape_squeeze.3 = bf16[1280,2048]{1,0:T(8,128)(2,1)} reshape(bf16[128,1,10,2048]{3,2,1,0:T(8,128)(2,1)} %all_to_all.26) | data formatting | bytes 10485760 | tf_op jit(solution)/shard_map/reshape;squeeze | solution.py:132
  538.9 7.4 %fusion.10 = f32[1280,704]{0,1:T(8,128)S(1)} fusion(bf16[1280,2048]{1,0:T(8,128)(2,1)} %reshape_squeeze.3, bf16[1,2048,704]{1,2,0:T(8,128)(2,1)} %param.34), kind=kOutput, calls=%fused_computation.31 | convolution fusion | flops 3690987520 | bytes 11730944 | tf_op jit(solution)/shard_map/dot_general | solution.py:124
  546.4 4.2 fusion.6
  550.6 6.1 convolution_convert_fusion
  556.7 9.5 %stack_reshape.5 = bf16[128,1,10,2048]{3,2,0,1:T(8,128)(2,1)} reshape(bf16[1280,2048]{1,0:T(8,128)(2,1)} %convolution_convert_fusion) | data formatting | bytes 10485760 | tf_op jit(solution)/shard_map/stack;reshape | solution.py:135
  566.2 6.1 all-to-all-start.4
  572.8 1.3 fusion.15
  574.1 4.8 gather_fusion.5
  579.2 102.7 %all-to-all-done.4 = bf16[128,1,10,2048]{3,2,1,0:T(8,128)(2,1)} async-done(((bf16[128,1,10,2048]{3,2,1,0:T(8,128)(2,1)}), bf16[128,1,10,2048]{3,2,1,0:T(8,128)(2,1)}, u32[]{:S(2)}, u32[]{:S(2)}) %all-to-all-start.4) | async-done | bytes 5242912 | tf_op jit(solution)/shard_map/all_to_all | solution.py:276
  681.9 5.7 add_convert_fusion
  687.6 5.5 convert_element_type.181
  693.2 7.2 gather_fusion.2
  700.3 3.9 reshape.408
  704.2 3.8 multiply_reduce_fusion
  708.0 0.8 fusion.28
  (124 shorter events, 13.9 us)
Async XLA Ops:
  6.5 544.0 %copy-start = (bf16[1,704,2048]{2,1,0:T(8,128)(2,1)S(1)}, bf16[1,704,2048]{2,1,0:T(8,128)(2,1)}, u32[]{:S(2)}) copy-start(bf16[1,704,2048]{2,1,0:T(8,128)(2,1)} %param.36) | copy-start | bytes 8650756
  11.0 9.9 %all-to-all-start.2 = ((bf16[8,2,1,2048]{3,1,2,0:T(2,128)(2,1)}), bf16[8,2,1,2048]{3,1,2,0:T(2,128)(2,1)S(1)}, u32[]{:S(2)}, u32[]{:S(2)}) async-start(bf16[8,2,1,2048]{3,1,2,0:T(2,128)(2,1)} %bitcast.16), calls=%async_computation.2 | async-start | bytes 131072 | tf_op jit(solution)/shard_map/all_to_all | solution.py:182
  38.0 8.6 %copy-start.18 = (bf16[2048]{0:T(1024)(128)(2,1)S(1)}, bf16[2048]{0:T(1024)(128)(2,1)}, u32[]{:S(2)}) copy-start(bf16[2048]{0:T(1024)(128)(2,1)} %param.23) | copy-start | bytes 12292
  38.0 8.6 %copy-start.22 = (bf16[512]{0:T(512)(128)(2,1)S(1)}, bf16[512]{0:T(512)(128)(2,1)}, u32[]{:S(2)}) copy-start(bf16[512]{0:T(512)(128)(2,1)} %param.28) | copy-start | bytes 3076
  38.0 226.1 %all-to-all-start.1 = ((bf16[16,16,1,32,512]{4,3,2,1,0:T(8,128)(2,1)}), bf16[16,16,1,32,512]{4,3,2,1,0:T(8,128)(2,1)}, u32[]{:S(2)}, u32[]{:S(2)}) async-start(bf16[16,16,1,32,512]{4,3,2,1,0:T(8,128)(2,1)} %stack.3), calls=%async_computation.1 | async-start | bytes 16777216 | tf_op jit(solution)/shard_map/all_to_all | solution.py:188
  46.6 172.8 %all-gather.7.cloned.1.call-start = ((), (), s32[]{:S(2)}) async-start(), calls=%async_computation.6 | async-start | bytes 1253376 | tf_op jit(solution)/shard_map/all_gather | solution.py:217
  49.8 5.4 copy-start.4
  49.8 6.8 copy-start.10
  49.8 9.3 %copy-start.14 = (s32[16,16]{1,0:T(8,128)S(1)}, s32[16,16]{1,0:T(8,128)}, u32[]{:S(2)}) copy-start(s32[16,16]{1,0:T(8,128)} %param.41) | copy-start | bytes 3076
  53.2 2.0 copy-start.1
  55.2 8.9 %copy-start.9 = (bf16[2048,64]{0,1:T(8,128)(2,1)S(1)}, bf16[2048,64]{0,1:T(8,128)(2,1)}, u32[]{:S(2)}) copy-start(bf16[2048,64]{0,1:T(8,128)(2,1)} %param.27) | copy-start | bytes 786436
  56.5 188.4 %all-gather.5.cloned.1.call-start = ((), (), s32[]{:S(2)}) async-start(), calls=%async_computation.5 | async-start | bytes 1114112 | tf_op jit(solution)/shard_map/all_gather | solution.py:190
  58.5 0.6 copy-start.16
  63.5 0.6 copy-start.12
  64.1 2.1 copy-start.20
  65.4 146.5 %copy-start.13 = (f32[1040]{0:T(1024)S(1)}, f32[1040]{0:T(1024)}, u32[]{:S(2)}) copy-start(f32[1040]{0:T(1024)} %copy-done.12) | copy-start | bytes 12484
  207.7 4.2 copy-start.21
  208.1 10.5 %copy-start.7 = (bf16[1040,64]{0,1:T(8,128)(2,1)}, bf16[1040,64]{0,1:T(8,128)(2,1)S(1)}, u32[]{:S(2)}) copy-start(bf16[1040,64]{0,1:T(8,128)(2,1)S(1)} %reshape.481) | copy-start | bytes 399364
  260.4 1.4 copy-start.2
  282.6 2.3 copy-start.15
  285.4 1.2 copy-start.5
  285.4 1.5 copy-start.6
  286.9 1.8 slice-start
  293.1 4.2 copy-start.8
  297.3 81.8 %copy-start.19 = (bf16[2048]{0:T(1024)(128)(2,1)S(1)}, bf16[2048]{0:T(1024)(128)(2,1)}, u32[]{:S(2)}) copy-start(bf16[2048]{0:T(1024)(128)(2,1)} %param.32) | copy-start | bytes 12292
  297.4 81.8 %copy-start.23 = (u32[128]{0:T(128)S(1)}, u32[128]{0:T(128)}, u32[]{:S(2)}) copy-start(u32[128]{0:T(128)} %constant.195) | copy-start | bytes 1540
  369.8 15.2 %collective-permute-start.1 = (bf16[80,2048]{1,0:T(8,128)(2,1)S(1)}, bf16[80,2048]{1,0:T(8,128)(2,1)}, u32[]{:S(2)}, u32[]{:S(2)}) collective-permute-start(bf16[80,2048]{1,0:T(8,128)(2,1)S(1)} %fusion), channel_id=1, source_target_pairs={{0,2},{1,3},{2,4},{3,5},{4,6},{5,7},{6,8},{7,9},{8,10},{9,11},{10,... | collective-permute-start | bytes 983048
  373.2 17.7 %collective-permute-start = (bf16[80,2048]{1,0:T(8,128)(2,1)S(1)}, bf16[80,2048]{1,0:T(8,128)(2,1)}, u32[]{:S(2)}, u32[]{:S(2)}) collective-permute-start(bf16[80,2048]{1,0:T(8,128)(2,1)S(1)} %fusion), channel_id=1, source_target_pairs={{0,1},{1,2},{2,3},{3,4},{4,5},{5,6},{6,7},{7,8},{8,9},{9,10},{10,1... | collective-permute-start | bytes 983048
  375.2 9.8 %collective-permute-start.2 = (bf16[65,2048]{1,0:T(8,128)(2,1)}, bf16[65,2048]{1,0:T(8,128)(2,1)}, u32[]{:S(2)}, u32[]{:S(2)}) collective-permute-start(bf16[65,2048]{1,0:T(8,128)(2,1)} %slice.109), channel_id=1, source_target_pairs={{0,3},{1,4},{2,5},{3,6},{4,7},{5,8},{6,9},{7,10},{8,11},{9,12},{10... | collective-permute-start | bytes 798728
  538.9 7.4 %copy-start.3 = (bf16[1280,2048]{1,0:T(8,128)(2,1)S(1)}, bf16[1280,2048]{1,0:T(8,128)(2,1)}, u32[]{:S(2)}) copy-start(bf16[1280,2048]{1,0:T(8,128)(2,1)} %reshape_squeeze.3) | copy-start | bytes 15728644
  538.9 7.5 %copy-start.24 = (bf16[1,2048,704]{1,2,0:T(8,128)(2,1)S(1)}, bf16[1,2048,704]{1,2,0:T(8,128)(2,1)}, u32[]{:S(2)}) copy-start(bf16[1,2048,704]{1,2,0:T(8,128)(2,1)} %param.35) | copy-start | bytes 8650756
  566.2 6.3 copy-start.11
  566.2 6.6 copy-start.17
  566.2 115.7 %all-to-all-start.4 = ((bf16[128,1,10,2048]{3,2,1,0:T(8,128)(2,1)}), bf16[128,1,10,2048]{3,2,1,0:T(8,128)(2,1)}, u32[]{:S(2)}, u32[]{:S(2)}) async-start(bf16[128,1,10,2048]{3,2,1,0:T(8,128)(2,1)} %bitcast.120), calls=%async_computation.4 | async-start | bytes 16777216 | tf_op jit(solution)/shard_map/all_to_all | solution.py:276
Sparse Core Ops, SparseCore 0:
  56.6 125.9 all-gather.6
  184.8 60.0 all-gather.4
